TPU v7x, 512 devices: a whole 4x4x16 slice. The times are simulated.
512 devices in a mesh: group: 8 (over z_hi, y), dp: 8 (over z_lo), tensor: 8 (over x, core).
Axes of the slice: x: 4, y: 4, z: 16 (z_hi: 2, z_lo: 8; z = z_hi * 8 + z_lo), core: 2. Of those that a mesh axis runs over, the one named last changes fastest.
Arguments:
- hidden: bfloat16 [4, 4096, 5120], P(None, ('group', 'dp'), 'tensor'), may hold values from -6 to 6
- cache: bfloat16 [4096, 8, 128, 256], P(('group', 'dp'), 'tensor'), as said below
- lengths: int32 [4096], P(('group', 'dp')), may hold values from 1 to 128, as said below
- norm_gain: float32 [5120], replicated, may hold values from 0.1 to 1.9
- w_qkv: bfloat16 [5120, 5120], P(('group', 'dp'), 'tensor'), may hold values from -0.078125 to 0.078125
- qkv_bias: float32 [5120], P('tensor'), may hold values from -3 to 3
- w_out: bfloat16 [5120, 3072], P(('group', 'dp'), 'tensor'), may hold values from -0.109375 to 0.109375
Outputs:
- attended: bfloat16 [4, 4096, 5120], P(None, ('group', 'dp'), 'tensor')
Inputs may be any that keep to these rules, and one draw needn't show every extreme that they name: `cache`: the first 128 entries of the last dimension are keys, the rest values; positions at or beyond a sequence's length are never read. `lengths`: the first of each device's 64 sequences holds all 128 positions.
All inputs are finite; a program needn't handle non-finite values.
Results may differ from a plain program's by a relative error of at most 0.018.
Values may be sent and summed in bfloat16 or wider, within the bound.
A program may use at most 64 MiB of HBM per device.

v0:
```python
import jax
import jax.numpy as jnp
from jax import lax
from jax.sharding import PartitionSpec as P

ROPE_BASE = 1000000.0
NEG_FILL = -1e30
NORM_EPS = 1e-06


def rotate(vectors, places):
    half = vectors.shape[-1] // 2
    inverse = ROPE_BASE ** (-(jnp.arange(half, dtype=jnp.float32) * 2.0 / vectors.shape[-1]))
    angles = places[..., None] * inverse
    cosine = jnp.cos(angles)
    sine_part = jnp.sin(angles)
    first_half = vectors[..., :half]
    second_half = vectors[..., half:]
    return jnp.concatenate(
        [
            first_half * cosine - second_half * sine_part,
            second_half * cosine + first_half * sine_part,
        ],
        axis=-1,
    )


def attend(queries, new_keys, new_values, cached, lengths):
    head_size = queries.shape[-1]
    num_steps = queries.shape[0]
    span = cached.shape[2]
    score_scale = head_size ** (-0.5)
    cache_keys = cached[..., :head_size]
    cache_values = cached[..., head_size:]
    old_scores = (
        jnp.einsum("srhqd,rhcd->srhqc", queries, cache_keys, preferred_element_type=jnp.float32)
        * score_scale
    )
    live = jnp.arange(span, dtype=jnp.int32)[None, :] < lengths[:, None]
    old_scores = jnp.where(live[None, :, None, None, :], old_scores, NEG_FILL)
    fresh_scores = (
        jnp.einsum("srhqd,urhd->srhqu", queries, new_keys, preferred_element_type=jnp.float32)
        * score_scale
    )
    causal = (
        jnp.arange(num_steps, dtype=jnp.int32)[None, :]
        <= jnp.arange(num_steps, dtype=jnp.int32)[:, None]
    )
    fresh_scores = jnp.where(causal[:, None, None, None, :], fresh_scores, NEG_FILL)
    scores = jnp.concatenate([old_scores, fresh_scores], axis=-1)
    highest = jnp.max(scores, axis=-1, keepdims=True)
    weights = jnp.exp(scores - highest)
    weights = (weights / jnp.sum(weights, axis=-1, keepdims=True)).astype(jnp.bfloat16)
    mixed = jnp.einsum(
        "srhqc,rhcd->srhqd", weights[..., :span], cache_values, preferred_element_type=jnp.float32
    )
    mixed = mixed + jnp.einsum(
        "srhqu,urhd->srhqd", weights[..., span:], new_values, preferred_element_type=jnp.float32
    )
    return mixed.astype(jnp.bfloat16)


def on_device(hidden, cache, lengths, norm_gain, w_qkv, qkv_bias, w_out):
    whole = lax.all_gather(hidden, "tensor", axis=2, tiled=True)
    num_steps, num_rows, width = whole.shape
    local_heads = cache.shape[1]
    head_size = cache.shape[3] // 2
    group_size = w_out.shape[1] // (local_heads * head_size)
    source = whole.astype(jnp.float32).reshape(num_steps * num_rows, width)
    mean_square = jnp.mean(source * source, axis=-1, keepdims=True)
    normed = (source * lax.rsqrt(mean_square + NORM_EPS) * norm_gain).astype(jnp.bfloat16)
    projected = jnp.dot(
        normed,
        lax.all_gather(w_qkv, ("group", "dp"), axis=0, tiled=True),
        preferred_element_type=jnp.float32,
    )
    heads_projected = projected
    heads_projected = (heads_projected + qkv_bias).reshape(
        num_steps, num_rows, local_heads, group_size + 2, head_size
    )
    places = (lengths[None, :] + jnp.arange(num_steps, dtype=jnp.int32)[:, None]).astype(
        jnp.float32
    )
    queries = rotate(heads_projected[:, :, :, :group_size, :], places[:, :, None, None]).astype(
        jnp.bfloat16
    )
    new_keys = rotate(heads_projected[:, :, :, group_size, :], places[:, :, None]).astype(
        jnp.bfloat16
    )
    new_values = heads_projected[:, :, :, group_size + 1, :].astype(jnp.bfloat16)
    mixed = attend(queries, new_keys, new_values, cache, lengths)
    flat = mixed.reshape(num_steps * num_rows, local_heads * group_size * head_size)
    partial_value = lax.dot_general(
        flat,
        lax.all_gather(w_out, ("group", "dp"), axis=0, tiled=True),
        (((1,), (1,)), ((), ())),
        preferred_element_type=jnp.float32,
    )
    partial_value = partial_value.reshape(num_steps, num_rows, width)
    summed = lax.psum_scatter(
        partial_value.astype(jnp.bfloat16), "tensor", scatter_dimension=2, tiled=True
    )
    return summed


def solution(mesh):
    placed = (
        P(None, ("group", "dp"), "tensor"),
        P(("group", "dp"), "tensor", None, None),
        P(("group", "dp")),
        P(),
        P(("group", "dp"), "tensor"),
        P("tensor"),
        P(("group", "dp"), "tensor"),
    )
    return jax.shard_map(
        on_device,
        mesh=mesh,
        in_specs=placed,
        out_specs=P(None, ("group", "dp"), "tensor"),
        check_vma=False,
    )
```

profile of v0, /device:TPU:1, one launch (start us, length us, event | category | flops | bytes accessed | tf_op | source)
XLA Modules:
  0.0 943.7 jit_solution(12647277013152928700)
XLA Ops:
  6.5 0.7 all-gather.4.cloned.1.call-update
  7.3 0.7 all-gather.6.cloned.1.call-update
  8.1 0.7 all-gather.8.cloned.1.call-update
  8.8 0.7 iota_compare_fusion
  9.6 0.7 add_convert_fusion.1
  10.3 1.1 multiply_cosine_fusion.1
  11.4 37.9 %all-gather.4.cloned.1.call-done = bf16[4,64,5120]{2,1,0:T(8,128)(2,1)} async-done(((bf16[4,64,640]{2,1,0:T(8,128)(2,1)}), bf16[4,64,5120]{2,1,0:T(8,128)(2,1)}) %all-gather.4.cloned.1.call-update) | async-done | bytes 2621456 | tf_op jit(solution)/shard_map/all_gather | solution.py:64
  49.3 2.5 multiply_reduce_fusion
  51.9 3.0 fusion.1
  54.9 351.9 %all-gather.6.cloned.1.call-done = bf16[5120,640]{1,0:T(8,128)(2,1)} async-done(((bf16[80,640]{1,0:T(8,128)(2,1)}), bf16[5120,640]{1,0:T(8,128)(2,1)}) %all-gather.6.cloned.1.call-update) | async-done | bytes 6553616 | tf_op jit(solution)/shard_map/all_gather | solution.py:74
  406.8 5.9 convolution_add_fusion
  412.7 0.1 reshape.277
  412.8 0.1 slice.47
  412.9 0.1 slice.52
  413.2 1.2 fusion.33
  414.4 0.3 fusion.35
  414.7 0.6 fusion.18
  415.3 0.7 fusion.37
  416.0 1.4 fusion.36
  417.5 0.7 fusion.16
  418.1 0.5 divide_convert_fusion
  418.6 0.3 fusion.17
  419.0 0.7 fusion.11
  419.6 0.1 copy.27
  419.7 0.2 dot_general.28
  419.9 396.2 %all-gather.8.cloned.1.call-done = bf16[5120,384]{1,0:T(8,128)(2,1)} async-done(((bf16[80,384]{1,0:T(8,128)(2,1)}), bf16[5120,384]{1,0:T(8,128)(2,1)}) %all-gather.8.cloned.1.call-update) | async-done | bytes 3932176 | tf_op jit(solution)/shard_map/all_gather | solution.py:95
  816.1 3.7 convolution_convert_fusion
  819.8 5.8 copy.32
  825.6 8.4 reshape.287
  834.0 100.4 %reduce-scatter.4.cloned.1.call-done = bf16[640,256]{1,0:T(8,128)(2,1)} async-done(((bf16[5120,256]{1,0:T(8,128)(2,1)}), bf16[640,256]{1,0:T(8,128)(2,1)}) %reduce-scatter.4.cloned.1.call-update) | async-done | bytes 327696
  934.4 1.3 reshape.288
  935.7 1.4 copy.33
  (17 shorter events, 0.4 us)
Async XLA Ops:
  6.5 42.7 %all-gather.4.cloned.1.call-start = ((), (), s32[]{:S(2)}) async-start(), calls=%async_computation.1 | async-start | bytes 2949120 | tf_op jit(solution)/shard_map/all_gather | solution.py:64
  7.3 399.5 %all-gather.6.cloned.1.call-start = ((), (), s32[]{:S(2)}) async-start(), calls=%async_computation.2 | async-start | bytes 6656000 | tf_op jit(solution)/shard_map/all_gather | solution.py:74
  8.0 808.1 %all-gather.8.cloned.1.call-start = ((), (), s32[]{:S(2)}) async-start(), calls=%async_computation.3 | async-start | bytes 3993600 | tf_op jit(solution)/shard_map/all_gather | solution.py:95
  8.7 925.7 %reduce-scatter.4.cloned.1.call-start = ((), (), s32[]{:S(2)}) async-start(), calls=%async_computation.4 | async-start | bytes 2949120
  11.4 395.4 %copy-start.2 = (f32[640]{0:T(1024)S(1)}, f32[640]{0:T(1024)}, u32[]{:S(2)}) copy-start(f32[640]{0:T(1024)} %param.12) | copy-start | bytes 7684
  49.3 2.6 copy-start
  412.8 3.2 copy-start.1
Sparse Core Ops, SparseCore 0:
  9.5 39.7 all-gather.3
  51.4 355.3 all-gather.5
  408.9 407.1 all-gather.7
  834.1 100.2 reduce-scatter.3
where the time goes:
time: 945 us; the launch traced here: 944 us
  waiting for transfers between devices  889 us (94%)
  local copies, waits for them, and re-layouts  18 us (2%)
  between operations  13.3 us (1%)
  matrix products  12.6 us (1%)
  other arithmetic  11.1 us (1%)
    all_gather x1, waiting for transfers between devices, on_device(): lax.all_gather(w_out, ('group', 'dp'), axis=0, tiled=True)  396 us
    all_gather x1, waiting for transfers between devices, on_device(): lax.all_gather(w_qkv, ('group', 'dp'), axis=0, tiled=True)  352 us
    unnamed x5, waiting for transfers between devices  103 us
    all_gather x1, waiting for transfers between devices, on_device(): whole = lax.all_gather(hidden, 'tensor', axis=2, tiled=True)  37.9 us
  transfers between devices with their start and end apart: 4, of which 4 were waited for; matrix products, arithmetic and copies ran while one was open for 2% of the time, Pallas kernels for 0%

commit v1 on v0

v1 whole, which is shorter than its diff:
```python
import functools

import jax
import jax.numpy as jnp
import numpy as np
from jax import lax
from jax.experimental import pallas as pl
from jax.experimental.pallas import tpu as pltpu
from jax.sharding import PartitionSpec as P

MESH = pl.DeviceIdType.MESH
BF, F32 = jnp.bfloat16, jnp.float32
NT = (((1,), (1,)), ((), ()))
ROPE_BASE = 1000000.0
NEG = -1e30
EPS = 1e-6
NY, NZ, NX = 4, 16, 4
ROWS = 64
STEPS = 4
TOK = STEPS * ROWS
HD = 128
QPK = 3
DEEP = 80
FEAT = 640
OUTC = QPK * HD
ACUT = 48
OFFS = (0, 1, 3, 2)


def kernel(
    hidden_ref, cache_ref, lens_ref, gain_ref, wq_ref, bias_ref, wo_ref, freq_ref, out_ref,
    hid, cache, hg, xs, wq, wo, ssb, ps, pr, osb, orb, xsb, xrb, qs, sc, mx, rope_c, rope_s, rcol, acc,
    loc_sem, h1, hx, hs, hh, hsend, zs, zsend, ss_sem, rs, rss, oa, ob, oby, oy, osend, od, ods, xr, xss,
):
    g, d, t = lax.axis_index("group"), lax.axis_index("dp"), lax.axis_index("tensor")
    y, z = lax.rem(g, 4), (g // 4) * 8 + d
    x, c = t // 2, lax.rem(t, 2)

    def dev(dy=0, dz=0, dx=0, flip=False):
        yy, zz, xx = lax.rem(y + dy + NY, NY), lax.rem(z + dz + NZ, NZ), lax.rem(x + dx + NX, NX)
        return ((zz // 8) * 4 + yy, lax.rem(zz, 8), 2 * xx + ((1 - c) if flip else c))

    def slot(dy=0, dz=0):
        yy, zz = lax.rem(y + dy + NY, NY), lax.rem(z + dz + NZ, NZ)
        return ((zz // 8) * 4 + yy) * 8 + lax.rem(zz, 8)

    def send(src, dst, ssem, rsem, where):
        pltpu.make_async_remote_copy(
            src_ref=src, dst_ref=dst, send_sem=ssem, recv_sem=rsem, device_id=where, device_id_type=MESH
        ).start()

    def wait(ref, sem):
        pltpu.make_async_copy(ref, ref, sem).wait()

    loads = [
        pltpu.make_async_copy(hidden_ref, hid, loc_sem.at[0]),
        pltpu.make_async_copy(wq_ref, wq.at[z], loc_sem.at[1]),
        pltpu.make_async_copy(wo_ref, wo.at[slot()], loc_sem.at[2]),
        pltpu.make_async_copy(cache_ref, cache, loc_sem.at[3]),
    ]
    for copy in loads:
        copy.start()
    barrier = pltpu.get_barrier_semaphore()
    friends = [dev(dy=1), dev(dy=2), dev(dy=3), dev(dz=1), dev(dz=-1), dev(flip=True)]
    for dx in (1, 2, 3):
        friends += [dev(dx=dx), dev(dx=dx, flip=True)]
    for friend in friends:
        pl.semaphore_signal(barrier, inc=1, device_id=friend, device_id_type=MESH)

    hub = (c == lax.rem(y, 2)) & (lax.rem(x, 2) == y // 2)
    relay = (c == lax.rem(y, 2)) & (lax.rem(x, 2) != y // 2)
    leaf = c != lax.rem(y, 2)
    kb = x // 2

    loads[0].wait()
    ones = jnp.ones((8, FEAT), F32)
    for s in range(STEPS):
        raw = hid[s].astype(F32)
        hg[s * ROWS : (s + 1) * ROWS, :] = (raw * gain_ref[...]).astype(BF)
        ssb[t, :, s * ROWS : (s + 1) * ROWS] = lax.dot_general(
            ones, raw * raw, NT, preferred_element_type=F32, precision=lax.Precision.HIGHEST
        )

    @pl.when(hub)
    def _():
        xs[kb, y] = hg[...]

    loads[1].wait()
    pl.semaphore_wait(barrier, len(friends))

    cuts = ((0, ACUT), (ACUT, DEEP - ACUT))

    def z_send(way, zz, piece, k):
        lo, n = cuts[piece]
        ref = wq.at[zz, pl.ds(lo, n)]
        send(ref, ref, zsend, zs.at[way, k - 1, piece], dev(dz=1 if way == 0 else -1))

    def z_step(k):
        for piece in (0, 1):
            for way in (0, 1):
                if k == 8 and piece != way:
                    continue
                zz = lax.rem(z + (NZ - k if way == 0 else k), NZ)
                lo, n = cuts[piece]
                wait(wq.at[zz, pl.ds(lo, n)], zs.at[way, k - 1, piece])
                if k < 7 or (k == 7 and piece == way):
                    z_send(way, zz, piece, k + 1)

    def h_order(j):
        return lax.rem(y + OFFS[j], NY)

    def hub_event(j):
        @pl.when(hub)
        def _():
            ys = h_order(j)
            block = xs.at[kb, ys]
            if j:
                wait(block, h1.at[ys])
            send(block, block, hsend.at[0], hx.at[kb, ys], dev(dx=1))
            send(block, block, hsend.at[0], hx.at[kb, ys], dev(dx=-1))
            send(block, block, hsend.at[1], hs.at[kb, ys], dev(flip=True))

    def relay_event(j):
        @pl.when(relay)
        def _():
            ys = h_order(j)
            for side in (-1, 1):
                kbs = lax.rem(x + side + NX, NX) // 2
                block = xs.at[kbs, ys]
                wait(block, hx.at[kbs, ys])
                half = 0 if side == -1 else 1
                part = xs.at[kbs, ys, pl.ds(half * (TOK // 2), TOK // 2)]
                send(part, part, hsend.at[0], hh.at[half, ys], dev(dx=-side))
                send(block, block, hsend.at[1], hs.at[kbs, ys], dev(flip=True))

    def far_event(j):
        @pl.when(hub)
        def _():
            ys = h_order(j)
            for half in (0, 1):
                wait(xs.at[1 - kb, ys, pl.ds(half * (TOK // 2), TOK // 2)], hh.at[half, ys])
            block = xs.at[1 - kb, ys]
            send(block, block, hsend.at[1], hs.at[1 - kb, ys], dev(flip=True))

    def o_y(ref):
        for dy in (2, 1, 3):
            send(ref, ref, osend, oy, dev(dy=dy))

    def o_zsend(way, ref, sem):
        send(ref, ref, osend, sem, dev(dz=1 if way == 0 else -1))

    def o_start():
        part = wo.at[slot(), pl.ds(ACUT, DEEP - ACUT)]
        for j in (3, 1, 2):
            send(part, part, osend, oby.at[j], dev(dy=OFFS[j]))
        for way in (0, 1):
            o_zsend(way, part, ob.at[way, 0, 0])
        part = wo.at[slot(), pl.ds(0, ACUT)]
        for way in (0, 1):
            o_zsend(way, part, oa.at[way, 0])
        o_y(part)

    def o_rows():
        for j in (1, 2, 3):
            part = wo.at[slot(dy=-OFFS[j]), pl.ds(ACUT, DEEP - ACUT)]
            wait(part, oby.at[j])
            for way in (0, 1):
                o_zsend(way, part, ob.at[way, j, 0])

    acuts = ((0, 32), (32, 16))
    bcuts = ((ACUT, 16), (ACUT + 16, 16))

    def o_step(k):
        for way in (0, 1):
            home = slot(dz=-k if way == 0 else k)
            lo, n = acuts[way] if k == 8 else (0, ACUT)
            wait(wo.at[home, pl.ds(lo, n)], oa.at[way, k - 1])
            if k < 8:
                lo, n = acuts[way] if k == 7 else (0, ACUT)
                o_zsend(way, wo.at[home, pl.ds(lo, n)], oa.at[way, k])
        for j in range(4):
            for way in (0, 1):
                home = slot(dy=-OFFS[j], dz=-k if way == 0 else k)
                lo, n = bcuts[way] if k == 8 else (ACUT, DEEP - ACUT)
                wait(wo.at[home, pl.ds(lo, n)], ob.at[way, j, k - 1])
                if k < 8:
                    lo, n = bcuts[way] if k == 7 else (ACUT, DEEP - ACUT)
                    o_zsend(way, wo.at[home, pl.ds(lo, n)], ob.at[way, j, k])
        for way in (0, 1):
            if k < 8 or way == 0:
                o_y(wo.at[slot(dz=-k if way == 0 else k), pl.ds(0, ACUT)])

    for piece in (0, 1):
        for way in (0, 1):
            z_send(way, z, piece, 1)

    @pl.when(jnp.logical_not(hub))
    def _():
        yt = lax.rem(t, NY)
        send(hg, xs.at[kb, y], hsend.at[2], h1.at[y], dev(dy=yt - y))

    hub_event(0)
    for friend in friends[5:]:
        send(ssb.at[t], ssb.at[t], ss_sem.at[0], ss_sem.at[1], friend)
    loads[2].wait()

    eye = (
        lax.broadcasted_iota(jnp.int32, (ROWS, ROWS), 0) == lax.broadcasted_iota(jnp.int32, (ROWS, ROWS), 1)
    ).astype(BF)
    lens_b = lax.dot_general(
        eye,
        jnp.broadcast_to(lens_ref[...].astype(F32), (HD, ROWS)).astype(BF),
        NT,
        preferred_element_type=F32,
    )
    lane = lax.broadcasted_iota(jnp.int32, (ROWS, HD), 1)
    for s in range(STEPS):
        angle = (lens_b + float(s)) * freq_ref[...]
        rope_c[s * ROWS : (s + 1) * ROWS, :] = jnp.cos(angle)
        sine = jnp.sin(angle)
        rope_s[s * ROWS : (s + 1) * ROWS, :] = jnp.where(lane < HD // 2, -sine, sine)

    for k in range(1, 9):
        z_step(k)
        if k == 2:
            hub_event(1)
            relay_event(0)
        if k == 3:
            hub_event(2)
            hub_event(3)
            relay_event(1)
            o_start()
        if k == 4:
            far_event(0)
            o_rows()
        if k == 5:
            relay_event(2)
            far_event(1)
            o_step(1)
        if k == 6:
            relay_event(3)
            far_event(2)
        if k == 7:
            far_event(3)
            o_step(2)

    @pl.when(leaf)
    def _():
        for j in range(4):
            for kk in (0, 1):
                wait(xs.at[kk, h_order(j)], hs.at[kk, h_order(j)])

    def product(ys):
        total = jnp.zeros((TOK, FEAT), F32)
        for kk in (0, 1):
            total += jnp.dot(
                xs[kk, ys], wq[kk * 8 : (kk + 1) * 8].reshape(8 * DEEP, FEAT), preferred_element_type=F32
            )
        return total

    for j, dy in enumerate((2, 1, 3)):
        ps[j] = product(lax.rem(y + dy, NY)).astype(BF)
        send(ps.at[j], pr.at[j], rss.at[j], rs.at[j], dev(dy=dy))
    acc[...] = product(y)

    wait(ssb.at[0:7], ss_sem.at[1])
    whole = jnp.sum(ssb[...], axis=0)[0:1, :] * (1.0 / (8 * FEAT))
    scale = lax.rsqrt(whole + EPS)
    eye_t = (
        lax.broadcasted_iota(jnp.int32, (TOK, TOK), 0) == lax.broadcasted_iota(jnp.int32, (TOK, TOK), 1)
    ).astype(F32)
    rcol[...] = lax.dot_general(
        eye_t,
        jnp.broadcast_to(scale, (HD, TOK)),
        NT,
        preferred_element_type=F32,
        precision=lax.Precision.HIGHEST,
    )
    o_step(3)
    o_step(4)
    for j in (1, 2, 0):
        wait(pr.at[j], rs.at[j])
        acc[...] += pr[j].astype(F32)

    def head(i):
        cols = slice(i * HD, (i + 1) * HD)
        return acc[:, cols] * rcol[...] + bias_ref[:, cols]

    def rotate(v):
        return v * rope_c[...] + pltpu.roll(v, HD // 2, 1) * rope_s[...]

    for i in range(QPK):
        qs[i * TOK : (i + 1) * TOK, :] = rotate(head(i)).astype(BF).astype(F32)
    new_k = rotate(head(QPK)).astype(BF)
    new_v = head(QPK + 1).astype(BF)
    o_step(5)

    loads[3].wait()
    nq = STEPS * QPK

    def old_scores(r, _):
        q = qs[pl.ds(r, nq, stride=ROWS), :].astype(BF)
        sc[pl.ds(r, nq, stride=ROWS), :] = lax.dot_general(
            q, cache[r, :, 0:HD], NT, preferred_element_type=F32
        )
        return _

    lax.fori_loop(0, ROWS, old_scores, 0, unroll=8)
    factor = HD ** (-0.5)
    live = lax.broadcasted_iota(jnp.int32, (ROWS, HD), 1).astype(F32) < lens_b
    row = lax.broadcasted_iota(jnp.int32, (ROWS, TOK), 0)
    col = lax.broadcasted_iota(jnp.int32, (ROWS, TOK), 1)
    mine = lax.rem(col, ROWS) == row
    for i in range(nq):
        s = i % STEPS
        rows = slice(i * ROWS, (i + 1) * ROWS)
        old = jnp.where(live, sc[rows, :] * factor, NEG)
        fresh = (
            lax.dot_general(qs[rows, :].astype(BF), new_k, NT, preferred_element_type=F32) * factor
        )
        fresh = jnp.where(mine & (col < (s + 1) * ROWS), fresh, NEG)
        top = jnp.maximum(jnp.max(old, axis=1, keepdims=True), jnp.max(fresh, axis=1, keepdims=True))
        old = jnp.exp(old - top)
        fresh = jnp.exp(fresh - top)
        total = jnp.sum(old, axis=1, keepdims=True) + jnp.sum(fresh, axis=1, keepdims=True)
        sc[rows, :] = (old / total).astype(BF).astype(F32)
        mx[rows, :] = jnp.dot((fresh / total).astype(BF), new_v, preferred_element_type=F32)

    def old_values(r, _):
        p = sc[pl.ds(r, nq, stride=ROWS), :].astype(BF)
        mx[pl.ds(r, nq, stride=ROWS), :] += jnp.dot(p, cache[r, :, HD:], preferred_element_type=F32)
        return _

    o_step(6)
    lax.fori_loop(0, ROWS, old_values, 0, unroll=8)
    mixed = jnp.concatenate([mx[i * TOK : (i + 1) * TOK, :].astype(BF) for i in range(QPK)], axis=1)
    o_step(7)
    o_step(8)
    wait(wo.at[0:48, pl.ds(0, ACUT)], oy)

    def partial_out(index):
        block = wo[pl.ds(index * 8, 8)].reshape(8 * DEEP, OUTC)
        return lax.dot_general(mixed, block, NT, preferred_element_type=F32)

    for j, dx in enumerate((2, 1, 3, 0)):
        osb[j] = partial_out(2 * lax.rem(x + dx, NX) + 1 - c).astype(BF)
        send(osb.at[j], orb.at[j], ods.at[j], od.at[j], dev(flip=True))
    for j, dx in enumerate((2, 1, 3, 0)):
        total = partial_out(2 * lax.rem(x + dx, NX) + c)
        wait(orb.at[j], od.at[j])
        total += orb[j].astype(F32)
        if j < 3:
            xsb[j] = total.astype(BF)
            send(xsb.at[j], xrb.at[j], xss.at[j], xr.at[j], dev(dx=dx))
        else:
            acc[...] = total
    for j in (1, 2, 0):
        wait(xrb.at[j], xr.at[j])
        acc[...] += xrb[j].astype(F32)
    out_ref[...] = acc[...].astype(BF).reshape(STEPS, ROWS, FEAT)

    wait(wq.at[0:15], zsend)
    wait(wo.at[0:63], osend)
    wait(ssb.at[0:7], ss_sem.at[0])

    @pl.when(hub)
    def _():
        wait(xs, hsend.at[0])

    @pl.when(relay)
    def _():
        wait(xs.at[0], hsend.at[0])

    @pl.when(jnp.logical_not(leaf))
    def _():
        wait(xs, hsend.at[1])

    @pl.when(jnp.logical_not(hub))
    def _():
        wait(hg, hsend.at[2])

    for j in range(3):
        wait(ps.at[j], rss.at[j])
        wait(xsb.at[j], xss.at[j])
    for j in range(4):
        wait(osb.at[j], ods.at[j])


def on_device(hidden, cache, lengths, norm_gain, w_qkv, qkv_bias, w_out):
    t = lax.axis_index("tensor")
    gain = lax.dynamic_slice_in_dim(norm_gain, t * FEAT, FEAT).reshape(1, FEAT)
    half = np.arange(HD // 2, dtype=np.float32) * np.float32(2.0 / HD)
    freq = np.power(np.float32(ROPE_BASE), -half).astype(np.float32)
    freq = jnp.asarray(np.concatenate([freq, freq])[None, :])
    dma = pltpu.SemaphoreType.DMA
    vmem, hbm = pl.BlockSpec(memory_space=pltpu.VMEM), pl.BlockSpec(memory_space=pl.ANY)
    nq = STEPS * QPK * ROWS
    return pl.pallas_call(
        kernel,
        out_shape=jax.ShapeDtypeStruct((STEPS, ROWS, FEAT), BF),
        in_specs=[hbm, hbm, vmem, vmem, hbm, vmem, hbm, vmem],
        out_specs=vmem,
        scratch_shapes=[
            pltpu.VMEM((STEPS, ROWS, FEAT), BF),
            pltpu.VMEM((ROWS, 128, 2 * HD), BF),
            pltpu.VMEM((TOK, FEAT), BF),
            pltpu.VMEM((2, NY, TOK, FEAT), BF),
            pltpu.VMEM((NZ, DEEP, FEAT), BF),
            pltpu.VMEM((NY * NZ, DEEP, OUTC), BF),
            pltpu.VMEM((8, 8, TOK), F32),
            pltpu.VMEM((3, TOK, FEAT), BF),
            pltpu.VMEM((3, TOK, FEAT), BF),
            pltpu.VMEM((4, TOK, FEAT), BF),
            pltpu.VMEM((4, TOK, FEAT), BF),
            pltpu.VMEM((3, TOK, FEAT), BF),
            pltpu.VMEM((3, TOK, FEAT), BF),
            pltpu.VMEM((nq, HD), F32),
            pltpu.VMEM((nq, HD), F32),
            pltpu.VMEM((nq, HD), F32),
            pltpu.VMEM((TOK, HD), F32),
            pltpu.VMEM((TOK, HD), F32),
            pltpu.VMEM((TOK, HD), F32),
            pltpu.VMEM((TOK, FEAT), F32),
            dma((4,)),
            dma((NY,)),
            dma((2, NY)),
            dma((2, NY)),
            dma((2, NY)),
            dma((3,)),
            dma((2, 8, 2)),
            dma,
            dma((2,)),
            dma((3,)),
            dma((3,)),
            dma((2, 8)),
            dma((2, 4, 8)),
            dma((4,)),
            dma,
            dma,
            dma((4,)),
            dma((4,)),
            dma((3,)),
            dma((3,)),
        ],
        compiler_params=pltpu.CompilerParams(
            collective_id=0, has_side_effects=True, vmem_limit_bytes=56 * 2**20
        ),
    )(
        hidden,
        cache.reshape(ROWS, 128, 2 * HD),
        lengths.reshape(1, ROWS),
        gain,
        w_qkv,
        qkv_bias.reshape(1, FEAT),
        w_out,
        freq,
    )


def solution(mesh):
    placed = (
        P(None, ("group", "dp"), "tensor"),
        P(("group", "dp"), "tensor", None, None),
        P(("group", "dp")),
        P(),
        P(("group", "dp"), "tensor"),
        P("tensor"),
        P(("group", "dp"), "tensor"),
    )
    return jax.shard_map(
        on_device,
        mesh=mesh,
        in_specs=placed,
        out_specs=P(None, ("group", "dp"), "tensor"),
        check_vma=False,
    )
```

time: 945 us -> 109 us (0.12)
  waiting for transfers between devices: 889 us -> 0 us
  Pallas kernels: 0 us -> 104 us
  local copies, waits for them, and re-layouts: 18 us -> 4.35 us
  between operations: 13.3 us -> 0.01 us
  matrix products: 12.6 us -> 0 us
  other arithmetic: 11.1 us -> 0 us
    all_gather x3 -> x0, waiting for transfers between devices: 786 us -> none  [the longest x1 396 us: on_device(): lax.all_gather(w_out, ('group', 'dp'), axis=0, tiled=True)]
    pallas_call x0 -> x1, Pallas kernels: none -> 104 us  [on_device(): pl.pallas_call(kernel, out_shape=jax.ShapeDtypeStruct((STEPS, ROWS, FEAT)...]
    unnamed x5 -> x0, waiting for transfers between devices: 103 us -> none
    unnamed x11 -> x1, local copies, waits for them, and re-layouts: 17 us -> 1.73 us
    dot_general x6 -> x0, matrix products: 12.6 us -> none  [the longest x1 5.86 us: on_device(): jnp.dot(normed, lax.all_gather(w_qkv, ('group', 'dp'), axis=0, tiled=True...]
  transfers between devices with their start and end apart: 4 -> 0, of which waited for: 4 -> 0; matrix products, arithmetic and copies ran while one was open for 2% -> 0% of each run, Pallas kernels for 0% -> 0%
where the time goes in v1:
time: 109 us
  Pallas kernels  104 us (95%)
  local copies, waits for them, and re-layouts  4.35 us (4%)
    pallas_call x1, Pallas kernels, on_device(): pl.pallas_call(kernel, out_shape=jax.ShapeDtypeStruct((STEPS, ROWS, FEAT)...  104 us

profile of v1, /device:TPU:1, one launch (start us, length us, event | category | flops | bytes accessed | tf_op | source)
XLA Modules:
  0.0 108.8 jit_solution(12899027148331527102)
XLA Ops:
  0.0 1.3 %reshape.15.bias_ref = f32[1,640]{1,0:T(1,128)} reshape(f32[640]{0:T(1024)} %param.13) | data formatting | bytes 5120 | tf_op jit(solution)/shard_map/reshape | solution.py:454
  1.3 0.8 dynamic_slice.3
  2.0 0.6 reshape.14.gain_ref
  2.6 104.4 %shard_map.82 = bf16[4,64,640]{2,1,0:T(8,128)(2,1)} custom-call(bf16[4,64,640]{2,1,0:T(8,128)(2,1)} %hidden_ref.1, bf16[64,128,256]{2,1,0:T(8,128)(2,1)} %bitcast.2, s32[1,64]{1,0:T(1,128)} %bitcast.3, f32[1,640]{1,0:T(1,128)} %reshape.14.gain_ref, bf16[80,640]{1,0:T(8,128)(2,1)} %wq_ref.1, f32[1,640]{1,0:T(1,128)} %reshape.15.bias_ref, ...), custom_call_target="tpu_custom_call" | custom-call | tf_op jit(solution)/shard_map/pallas_call | solution.py:398
  107.1 1.7 %copy.10 = bf16[4,64,640]{2,1,0:T(8,128)(2,1)} copy(bf16[4,64,640]{2,1,0:T(8,128)(2,1)} %shard_map.82) | data formatting | bytes 655360

commit v2 on v1

v2 whole, which is shorter than its diff:
```python
import functools

import jax
import jax.numpy as jnp
import numpy as np
from jax import lax
from jax.experimental import pallas as pl
from jax.experimental.pallas import tpu as pltpu
from jax.sharding import PartitionSpec as P

MESH = pl.DeviceIdType.MESH
BF, F32 = jnp.bfloat16, jnp.float32
NT = (((1,), (1,)), ((), ()))
ROPE_BASE = 1000000.0
NEG = -1e30
EPS = 1e-6
NY, NZ, NX = 4, 16, 4
ROWS = 64
STEPS = 4
TOK = STEPS * ROWS
HD = 128
HALF = 32
HTOK = STEPS * HALF
QPK = 3
DEEP = 80
FEAT = 640
OUTC = QPK * HD
ACUT = 64
ZCUTS = ((0, 32), (32, 32), (64, 16))
OFFS = (0, 1, 3, 2)
PLAN = {
    1: [("oa", 1), ("oy", 1), ("of", 0), ("hub", 1, 0), ("hub", 2, 0), ("relay", 0, 0)],
    2: [("oa", 2), ("oy", 2), ("of", 1), ("hub", 1, 1), ("hub", 2, 1), ("hub", 3, 0), ("relay", 0, 1), ("ob", 0)],
    3: [("oa", 3), ("oy", 3), ("of", 2), ("hub", 3, 1), ("relay", 1, 0), ("relay", 2, 0), ("far", 0, 0), ("far", 0, 1), ("rope", 0, 0), ("rope", 0, 1)],
    4: [("oa", 4), ("oy", 4), ("of", 3), ("relay", 1, 1), ("relay", 2, 1), ("far", 1, 0), ("far", 2, 0), ("rope", 0, 2), ("rope", 0, 3), ("ob", 1)],
    5: [("oa", 5), ("oy", 5), ("of", 4), ("relay", 3, 0), ("relay", 3, 1), ("rope", 1, 0), ("rope", 1, 1), ("ob", 2)],
    6: [("oa", 6), ("oy", 6), ("of", 5), ("far", 1, 1), ("far", 2, 1), ("far", 3, 0), ("far", 3, 1), ("rope", 1, 2), ("rope", 1, 3), ("ob", 3)],
    7: [("oa", 7), ("oy", 7), ("of", 6), ("ob", 4)],
    8: [("oa", 8), ("oy", 8), ("of", 7), ("ob", 5)],
    "sent": [("of", 8), ("ob", 6)],
    "back": [("ob", 7)],
    "first": [("ob", 8)],
}


def kernel(
    hidden_ref, cache_ref, lens_ref, gain_ref, wq_ref, bias_ref, wo_ref, freq_ref, out_ref,
    gain, bias, lens, freq, hid, cache, hg, xs, wq, wo, ssb, ps, pr, osb, orb, xsb, xrb, qs, sc, mx, rope_c, rope_s, rcol, acc,
    loc_sem, h1, hx, hs, hh, hsend, zs, zsend, ss_sem, rs, rss, oa, ob, oby, oyf, oy, osend, od, ods, xr, xss,
):
    g, d, t = lax.axis_index("group"), lax.axis_index("dp"), lax.axis_index("tensor")
    y, z = lax.rem(g, 4), (g // 4) * 8 + d
    x, c = t // 2, lax.rem(t, 2)

    def dev(dy=0, dz=0, dx=0, flip=False):
        yy, zz, xx = lax.rem(y + dy + NY, NY), lax.rem(z + dz + NZ, NZ), lax.rem(x + dx + NX, NX)
        return ((zz // 8) * 4 + yy, lax.rem(zz, 8), 2 * xx + ((1 - c) if flip else c))

    def slot(dy=0, dz=0):
        yy, zz = lax.rem(y + dy + NY, NY), lax.rem(z + dz + NZ, NZ)
        return ((zz // 8) * 4 + yy) * 8 + lax.rem(zz, 8)

    def send(src, dst, ssem, rsem, where):
        pltpu.make_async_remote_copy(
            src_ref=src, dst_ref=dst, send_sem=ssem, recv_sem=rsem, device_id=where, device_id_type=MESH
        ).start()

    def wait(ref, sem):
        pltpu.make_async_copy(ref, ref, sem).wait()

    loads = [
        pltpu.make_async_copy(hidden_ref, hid, loc_sem.at[0]),
        pltpu.make_async_copy(wq_ref, wq.at[z], loc_sem.at[1]),
        pltpu.make_async_copy(wo_ref, wo.at[slot()], loc_sem.at[2]),
        pltpu.make_async_copy(cache_ref, cache, loc_sem.at[3]),
        pltpu.make_async_copy(gain_ref, gain, loc_sem.at[4]),
        pltpu.make_async_copy(bias_ref, bias, loc_sem.at[5]),
        pltpu.make_async_copy(lens_ref, lens, loc_sem.at[6]),
        pltpu.make_async_copy(freq_ref, freq, loc_sem.at[7]),
    ]
    for copy in loads[1:2] + loads[:1] + loads[4:] + loads[2:4]:
        copy.start()
    barrier = pltpu.get_barrier_semaphore()
    friends = [dev(dy=1), dev(dy=2), dev(dy=3), dev(dz=1), dev(dz=-1), dev(flip=True)]
    for dx in (1, 2, 3):
        friends += [dev(dx=dx), dev(dx=dx, flip=True)]
    for friend in friends:
        pl.semaphore_signal(barrier, inc=1, device_id=friend, device_id_type=MESH)

    hub = (c == lax.rem(y, 2)) & (lax.rem(x, 2) == y // 2)
    relay = (c == lax.rem(y, 2)) & (lax.rem(x, 2) != y // 2)
    leaf = c != lax.rem(y, 2)
    kb = x // 2

    loads[1].wait()
    pl.semaphore_wait(barrier, len(friends))

    pieces = len(ZCUTS)

    def z_part(zz, piece):
        lo, n = ZCUTS[piece]
        return wq.at[zz, pl.ds(lo, n)]

    def z_send(way, zz, piece, k):
        send(z_part(zz, piece), z_part(zz, piece), zsend, zs.at[way, k - 1, piece], dev(dz=1 if way == 0 else -1))

    def z_last(way, piece):
        return (piece < pieces // 2) == (way == 1)

    def z_step(k):
        for piece in range(pieces):
            for way in (0, 1):
                if k == 8 and not z_last(way, piece):
                    continue
                zz = lax.rem(z + (NZ - k if way == 0 else k), NZ)
                wait(z_part(zz, piece), zs.at[way, k - 1, piece])
                if k < 7 or (k == 7 and z_last(way, piece)):
                    z_send(way, zz, piece, k + 1)

    def h_part(kbs, j, h, lo=0, n=HTOK):
        return xs.at[kbs, lax.rem(y + OFFS[j], NY), pl.ds(h * HTOK + lo, n)]

    def hub_event(j, h):
        @pl.when(hub)
        def _():
            part = h_part(kb, j, h)
            if j:
                wait(part, h1.at[j, h])
            send(part, part, hsend.at[0], hx.at[kb, j, h], dev(dx=1))
            send(part, part, hsend.at[0], hx.at[kb, j, h], dev(dx=-1))
            send(part, part, hsend.at[1], hs.at[kb, j, h], dev(flip=True))

    def relay_event(j, h):
        @pl.when(relay)
        def _():
            for side in (-1, 1):
                kbs = lax.rem(x + side + NX, NX) // 2
                part = h_part(kbs, j, h)
                wait(part, hx.at[kbs, j, h])
                far = 0 if side == -1 else 1
                piece = h_part(kbs, j, h, far * (HTOK // 2), HTOK // 2)
                send(piece, piece, hsend.at[0], hh.at[far, j, h], dev(dx=-side))
                send(part, part, hsend.at[1], hs.at[kbs, j, h], dev(flip=True))

    def far_event(j, h):
        @pl.when(hub)
        def _():
            for far in (0, 1):
                wait(h_part(1 - kb, j, h, far * (HTOK // 2), HTOK // 2), hh.at[far, j, h])
            part = h_part(1 - kb, j, h)
            send(part, part, hsend.at[1], hs.at[1 - kb, j, h], dev(flip=True))

    def o_y(k, way):
        part = wo.at[slot(dz=-k if way == 0 else k), pl.ds(0, ACUT)]
        send(part, part, osend, oyf.at[0, k] if way == 0 and k < 8 else oy, dev(dy=1))
        send(part, part, osend, oyf.at[1, k] if (way == 1 and k > 0) or k == 8 else oy, dev(dy=-1))

    def o_yfwd(k):
        for way in (0, 1):
            if k == 0 and way == 1 or k == 8 and way == 0:
                continue
            part = wo.at[slot(dy=-1 if way == 0 else 1, dz=-k if way == 0 else k), pl.ds(0, ACUT)]
            wait(part, oyf.at[way, k])
            send(part, part, osend, oy, dev(dy=1 if way == 0 else -1))

    def o_zsend(way, ref, sem):
        send(ref, ref, osend, sem, dev(dz=1 if way == 0 else -1))

    def o_start():
        part = wo.at[slot(), pl.ds(ACUT, DEEP - ACUT)]
        for j in (3, 1, 2):
            send(part, part, osend, oby.at[j], dev(dy=OFFS[j]))
        part = wo.at[slot(), pl.ds(0, ACUT)]
        for way in (0, 1):
            o_zsend(way, part, oa.at[way, 0])
        o_y(0, 0)

    def ob_start():
        for j in (0, 1, 2, 3):
            part = wo.at[slot(dy=-OFFS[j]), pl.ds(ACUT, DEEP - ACUT)]
            if j:
                wait(part, oby.at[j])
            for way in (0, 1):
                o_zsend(way, part, ob.at[way, j, 0])

    acuts = ((0, 32), (32, 32))

    def oa_step(k):
        for way in (0, 1):
            home = slot(dz=-k if way == 0 else k)
            lo, n = acuts[way] if k == 8 else (0, ACUT)
            wait(wo.at[home, pl.ds(lo, n)], oa.at[way, k - 1])
            if k < 8:
                lo, n = acuts[way] if k == 7 else (0, ACUT)
                o_zsend(way, wo.at[home, pl.ds(lo, n)], oa.at[way, k])

    def oa_y(k):
        for way in (0, 1):
            if k < 8 or way == 0:
                o_y(k, way)

    def ob_step(k):
        for j in range(4):
            for way in (0, 1):
                if k == 8 and j % 2 != way:
                    continue
                part = wo.at[slot(dy=-OFFS[j], dz=-k if way == 0 else k), pl.ds(ACUT, DEEP - ACUT)]
                wait(part, ob.at[way, j, k - 1])
                if k < 7 or (k == 7 and j % 2 == way):
                    o_zsend(way, part, ob.at[way, j, k])

    for piece in range(pieces):
        for way in (0, 1):
            z_send(way, z, piece, 1)
    loads[0].wait()
    loads[4].wait()
    for i in range(FEAT // HD):
        cols = slice(i * HD, (i + 1) * HD)
        row = gain[pl.ds(t * (FEAT // HD) + i, 1), :]
        for h in (0, 1):
            part = hid[:, h * HALF : (h + 1) * HALF, cols].reshape(HTOK, HD)
            hg[h * HTOK : (h + 1) * HTOK, cols] = (part.astype(F32) * row).astype(BF)

    @pl.when(hub)
    def _():
        xs[kb, y] = hg[...]

    back_y = lax.rem(y - lax.rem(t, NY) + NY, NY)
    order = lax.rem(back_y * (5 * back_y - 3) // 2, NY)

    @pl.when(jnp.logical_not(hub))
    def _():
        for h in (0, 1):
            rows = pl.ds(h * HTOK, HTOK)
            send(hg.at[rows], xs.at[kb, y, rows], hsend.at[2], h1.at[order, h], dev(dy=-back_y))

    hub_event(0, 0)
    hub_event(0, 1)
    loads[2].wait()
    o_start()
    ones = jnp.ones((8, FEAT), F32)
    for h in (0, 1):
        raw = hid[:, h * HALF : (h + 1) * HALF, :].reshape(HTOK, FEAT).astype(F32)
        ssb[t, :, h * HTOK : (h + 1) * HTOK] = lax.dot_general(
            ones, raw * raw, NT, preferred_element_type=F32, precision=lax.Precision.HIGHEST
        )
    for friend in friends[5:]:
        send(ssb.at[t], ssb.at[t], ss_sem.at[0], ss_sem.at[1], friend)

    eye = (
        lax.broadcasted_iota(jnp.int32, (ROWS, ROWS), 0) == lax.broadcasted_iota(jnp.int32, (ROWS, ROWS), 1)
    ).astype(BF)
    loads[6].wait()
    loads[7].wait()
    lens_b = lax.dot_general(
        eye,
        jnp.broadcast_to(lens[...].astype(F32), (HD, ROWS)).astype(BF),
        NT,
        preferred_element_type=F32,
    )
    lane = lax.broadcasted_iota(jnp.int32, (HALF, HD), 1)

    def rope_table(h, s):
        rows = slice((h * STEPS + s) * HALF, (h * STEPS + s + 1) * HALF)
        angle = (lens_b[h * HALF : (h + 1) * HALF, :] + float(s)) * freq[...]
        rope_c[rows, :] = jnp.cos(angle)
        sine = jnp.sin(angle)
        rope_s[rows, :] = jnp.where(lane < HD // 2, -sine, sine)

    events = {
        "hub": hub_event,
        "relay": relay_event,
        "far": far_event,
        "oa": oa_step,
        "oy": oa_y,
        "of": o_yfwd,
        "ob": lambda k: ob_step(k) if k else ob_start(),
        "rope": rope_table,
    }

    def run(key):
        for name, *what in PLAN[key]:
            events[name](*what)

    for k in range(1, 9):
        z_step(k)
        run(k)

    @pl.when(leaf)
    def _():
        for j in range(4):
            for kk in (0, 1):
                for h in (0, 1):
                    wait(h_part(kk, j, h), hs.at[kk, j, h])

    def product(ys):
        total = jnp.zeros((TOK, FEAT), F32)
        for kk in (0, 1):
            total += jnp.dot(
                xs[kk, ys], wq[kk * 8 : (kk + 1) * 8].reshape(8 * DEEP, FEAT), preferred_element_type=F32
            )
        return total

    def rows_of(h):
        return slice(h * HTOK, (h + 1) * HTOK)

    def r_send(j, dy, h):
        rows = pl.ds(h * HTOK, HTOK)
        send(ps.at[j, rows], pr.at[j, rows], rss.at[j, h], rs.at[j, h], dev(dy=dy))

    ways = ((0, 2), (1, 1), (2, 3))
    for j, dy in ways:
        ps[j] = product(lax.rem(y + dy, NY)).astype(BF)
        r_send(j, dy, 0)
    for j, dy in ways:
        r_send(j, dy, 1)
    acc[...] = product(y)
    run("sent")

    wait(ssb.at[0:7], ss_sem.at[1])
    whole = jnp.sum(ssb[...], axis=0)[0:1, :] * (1.0 / (8 * FEAT))
    scale = lax.rsqrt(whole + EPS)
    eye_t = (
        lax.broadcasted_iota(jnp.int32, (TOK, TOK), 0) == lax.broadcasted_iota(jnp.int32, (TOK, TOK), 1)
    ).astype(F32)
    rcol[...] = lax.dot_general(
        eye_t,
        jnp.broadcast_to(scale, (HD, TOK)),
        NT,
        preferred_element_type=F32,
        precision=lax.Precision.HIGHEST,
    )
    run("back")
    loads[5].wait()
    loads[3].wait()

    nq = STEPS * QPK
    factor = HD ** (-0.5)
    span = lax.broadcasted_iota(jnp.int32, (HALF, HD), 1).astype(F32)
    fresh_row = lax.broadcasted_iota(jnp.int32, (HALF, HTOK), 0)
    fresh_col = lax.broadcasted_iota(jnp.int32, (HALF, HTOK), 1)
    mine = lax.rem(fresh_col, HALF) == fresh_row

    def attention(h):
        rows = rows_of(h)
        for j in (1, 2, 0):
            wait(pr.at[j, pl.ds(h * HTOK, HTOK)], rs.at[j, h])

        def head(i):
            cols = slice(i * HD, (i + 1) * HD)
            total = acc[rows, cols]
            for j in range(3):
                total += pr[j, rows, cols].astype(F32)
            return total * rcol[rows, :] + bias[i : i + 1, :]

        def rotate(v):
            return v * rope_c[rows, :] + pltpu.roll(v, HD // 2, 1) * rope_s[rows, :]

        for i in range(QPK):
            qs[i * HTOK : (i + 1) * HTOK, :] = rotate(head(i)).astype(BF).astype(F32)
        new_k = rotate(head(QPK)).astype(BF)
        new_v = head(QPK + 1).astype(BF)

        def old_scores(r, carry):
            q = qs[pl.ds(r, nq, stride=HALF), :].astype(BF)
            sc[pl.ds(r, nq, stride=HALF), :] = lax.dot_general(
                q, cache[h * HALF + r, :, 0:HD], NT, preferred_element_type=F32
            )
            return carry

        lax.fori_loop(0, HALF, old_scores, 0, unroll=32)
        live = span < lens_b[h * HALF : (h + 1) * HALF, :]
        for i in range(nq):
            s = i % STEPS
            part = slice(i * HALF, (i + 1) * HALF)
            old = jnp.where(live, sc[part, :] * factor, NEG)
            fresh = lax.dot_general(qs[part, :].astype(BF), new_k, NT, preferred_element_type=F32)
            fresh = jnp.where(mine & (fresh_col < (s + 1) * HALF), fresh * factor, NEG)
            top = jnp.max(jnp.maximum(old, fresh), axis=1, keepdims=True)
            old = jnp.exp(old - top)
            fresh = jnp.exp(fresh - top)
            total = jnp.sum(old + fresh, axis=1, keepdims=True)
            sc[part, :] = (old / total).astype(BF).astype(F32)
            mx[part, :] = jnp.dot((fresh / total).astype(BF), new_v, preferred_element_type=F32)

        def old_values(r, carry):
            p = sc[pl.ds(r, nq, stride=HALF), :].astype(BF)
            mx[pl.ds(r, nq, stride=HALF), :] += jnp.dot(
                p, cache[h * HALF + r, :, HD:], preferred_element_type=F32
            )
            return carry

        lax.fori_loop(0, HALF, old_values, 0, unroll=32)
        return jnp.concatenate(
            [mx[i * HTOK : (i + 1) * HTOK, :].astype(BF) for i in range(QPK)], axis=1
        )

    def partial_out(mixed, index):
        block = wo[pl.ds(index * 8, 8)].reshape(8 * DEEP, OUTC)
        return lax.dot_general(mixed, block, NT, preferred_element_type=F32)

    def outputs(h, mixed):
        rows, there = rows_of(h), pl.ds(h * HTOK, HTOK)
        for j, dx in enumerate((2, 1, 3, 0)):
            osb[j, rows] = partial_out(mixed, 2 * lax.rem(x + dx, NX) + 1 - c).astype(BF)
            send(osb.at[j, there], orb.at[j, there], ods.at[j, h], od.at[j, h], dev(flip=True))
        for j, dx in enumerate((2, 1, 3, 0)):
            total = partial_out(mixed, 2 * lax.rem(x + dx, NX) + c)
            wait(orb.at[j, there], od.at[j, h])
            total += orb[j, rows].astype(F32)
            if j < 3:
                xsb[j, rows] = total.astype(BF)
                send(xsb.at[j, there], xrb.at[j, there], xss.at[j, h], xr.at[j, h], dev(dx=dx))
            else:
                acc[rows, :] = total

    def finish(h):
        rows = rows_of(h)
        for j in (1, 2, 0):
            wait(xrb.at[j, pl.ds(h * HTOK, HTOK)], xr.at[j, h])
        total = acc[rows, :]
        for j in range(3):
            total += xrb[j, rows].astype(F32)
        hid[:, h * HALF : (h + 1) * HALF, :] = total.astype(BF).reshape(STEPS, HALF, FEAT)

    mixed = attention(0)
    run("first")
    wait(wo.at[0:32, pl.ds(0, ACUT)], oy)
    outputs(0, mixed)
    mixed = attention(1)
    outputs(1, mixed)
    finish(0)
    finish(1)
    back = pltpu.make_async_copy(hid, out_ref, loc_sem.at[0])
    back.start()

    wait(wq.at[0:15], zsend)
    wait(wo.at[0:63], osend)
    wait(ssb.at[0:7], ss_sem.at[0])

    @pl.when(hub)
    def _():
        wait(xs, hsend.at[0])

    @pl.when(relay)
    def _():
        wait(xs.at[0], hsend.at[0])

    @pl.when(jnp.logical_not(leaf))
    def _():
        wait(xs, hsend.at[1])

    @pl.when(jnp.logical_not(hub))
    def _():
        wait(hg, hsend.at[2])

    for h in (0, 1):
        there = pl.ds(h * HTOK, HTOK)
        for j in range(3):
            wait(ps.at[j, there], rss.at[j, h])
            wait(xsb.at[j, there], xss.at[j, h])
        for j in range(4):
            wait(osb.at[j, there], ods.at[j, h])
    back.wait()


def on_device(hidden, cache, lengths, norm_gain, w_qkv, qkv_bias, w_out):
    half = np.arange(HD // 2, dtype=np.float32) * np.float32(2.0 / HD)
    freq = np.power(np.float32(ROPE_BASE), -half).astype(np.float32)
    freq = jnp.asarray(np.concatenate([freq, freq])[None, :])
    dma = pltpu.SemaphoreType.DMA
    hbm = pl.BlockSpec(memory_space=pl.ANY)
    nq = STEPS * QPK * HALF
    return pl.pallas_call(
        kernel,
        out_shape=jax.ShapeDtypeStruct((STEPS, ROWS, FEAT), BF),
        in_specs=[hbm] * 8,
        out_specs=hbm,
        scratch_shapes=[
            pltpu.VMEM((8 * FEAT // HD, HD), F32),
            pltpu.VMEM((FEAT // HD, HD), F32),
            pltpu.VMEM((1, ROWS), jnp.int32),
            pltpu.VMEM((1, HD), F32),
            pltpu.VMEM((STEPS, ROWS, FEAT), BF),
            pltpu.VMEM((ROWS, 128, 2 * HD), BF),
            pltpu.VMEM((TOK, FEAT), BF),
            pltpu.VMEM((2, NY, TOK, FEAT), BF),
            pltpu.VMEM((NZ, DEEP, FEAT), BF),
            pltpu.VMEM((NY * NZ, DEEP, OUTC), BF),
            pltpu.VMEM((8, 8, TOK), F32),
            pltpu.VMEM((3, TOK, FEAT), BF),
            pltpu.VMEM((3, TOK, FEAT), BF),
            pltpu.VMEM((4, TOK, FEAT), BF),
            pltpu.VMEM((4, TOK, FEAT), BF),
            pltpu.VMEM((3, TOK, FEAT), BF),
            pltpu.VMEM((3, TOK, FEAT), BF),
            pltpu.VMEM((nq, HD), F32),
            pltpu.VMEM((nq, HD), F32),
            pltpu.VMEM((nq, HD), F32),
            pltpu.VMEM((TOK, HD), F32),
            pltpu.VMEM((TOK, HD), F32),
            pltpu.VMEM((TOK, HD), F32),
            pltpu.VMEM((TOK, FEAT), F32),
            dma((8,)),
            dma((NY, 2)),
            dma((2, NY, 2)),
            dma((2, NY, 2)),
            dma((2, NY, 2)),
            dma((3,)),
            dma((2, 8, len(ZCUTS))),
            dma,
            dma((2,)),
            dma((3, 2)),
            dma((3, 2)),
            dma((2, 8)),
            dma((2, 4, 8)),
            dma((4,)),
            dma((2, 9)),
            dma,
            dma,
            dma((4, 2)),
            dma((4, 2)),
            dma((3, 2)),
            dma((3, 2)),
        ],
        compiler_params=pltpu.CompilerParams(
            collective_id=0, has_side_effects=True, vmem_limit_bytes=56 * 2**20
        ),
    )(
        hidden,
        cache.reshape(ROWS, 128, 2 * HD),
        lengths.reshape(1, ROWS),
        norm_gain.reshape(8 * FEAT // HD, HD),
        w_qkv,
        qkv_bias.reshape(FEAT // HD, HD),
        w_out,
        freq,
    )


def solution(mesh):
    placed = (
        P(None, ("group", "dp"), "tensor"),
        P(("group", "dp"), "tensor", None, None),
        P(("group", "dp")),
        P(),
        P(("group", "dp"), "tensor"),
        P("tensor"),
        P(("group", "dp"), "tensor"),
    )
    return jax.shard_map(
        on_device,
        mesh=mesh,
        in_specs=placed,
        out_specs=P(None, ("group", "dp"), "tensor"),
        check_vma=False,
    )
```

time: 109 us -> 92.6 us (0.85)
  Pallas kernels: 104 us -> 90.7 us
  local copies, waits for them, and re-layouts: 4.35 us -> 1.73 us
    pallas_call x1, Pallas kernels: 104 us -> 90.7 us  [on_device(): pl.pallas_call(kernel, out_shape=jax.ShapeDtypeStruct((STEPS, ROWS, FEAT)...]
    reshape x2 -> x0, local copies, waits for them, and re-layouts: 1.86 us -> none  [the longest x1 1.28 us: on_device(): qkv_bias.reshape(1, FEAT)]
where the time goes in v2:
time: 92.6 us; the launch traced here: 92.4 us
  Pallas kernels  90.7 us (98%)
  local copies, waits for them, and re-layouts  1.73 us (2%)
    pallas_call x1, Pallas kernels, on_device(): pl.pallas_call(kernel, out_shape=jax.ShapeDtypeStruct((STEPS, ROWS, FEAT)...  90.7 us

profile of v2, /device:TPU:1, one launch (start us, length us, event | category | flops | bytes accessed | tf_op | source)
XLA Modules:
  0.0 92.4 jit_solution(7077143238942234331)
XLA Ops:
  0.0 90.7 %shard_map.82 = bf16[4,64,640]{2,1,0:T(8,128)(2,1)} custom-call(bf16[4,64,640]{2,1,0:T(8,128)(2,1)} %hidden_ref.1, bf16[64,128,256]{2,1,0:T(8,128)(2,1)} %bitcast.4, s32[1,64]{1,0:T(1,128)} %bitcast.7, f32[40,128]{1,0:T(8,128)} %bitcast.5, bf16[80,640]{1,0:T(8,128)(2,1)} %wq_ref.1, f32[5,128]{1,0:T(8,128)} %bitcast.6, bf16[80,384]{1,0:T(8,128)(2,1)} %wo_ref.1, ...), custom_call_target="tpu_custom_call" | custom-call | tf_op jit(solution)/shard_map/pallas_call | solution.py:474
  90.7 1.7 %copy.10 = bf16[4,64,640]{2,1,0:T(8,128)(2,1)} copy(bf16[4,64,640]{2,1,0:T(8,128)(2,1)} %shard_map.82) | data formatting | bytes 655360

commit v3 on v2

--- a/solution.py
+++ b/solution.py
@@ -31,13 +31,13 @@
 PLAN = {
     1: [("oa", 1), ("oy", 1), ("of", 0), ("hub", 1, 0), ("hub", 2, 0), ("relay", 0, 0)],
     2: [("oa", 2), ("oy", 2), ("of", 1), ("hub", 1, 1), ("hub", 2, 1), ("hub", 3, 0), ("relay", 0, 1), ("ob", 0)],
-    3: [("oa", 3), ("oy", 3), ("of", 2), ("hub", 3, 1), ("relay", 1, 0), ("relay", 2, 0), ("far", 0, 0), ("far", 0, 1), ("rope", 0, 0), ("rope", 0, 1)],
-    4: [("oa", 4), ("oy", 4), ("of", 3), ("relay", 1, 1), ("relay", 2, 1), ("far", 1, 0), ("far", 2, 0), ("rope", 0, 2), ("rope", 0, 3), ("ob", 1)],
-    5: [("oa", 5), ("oy", 5), ("of", 4), ("relay", 3, 0), ("relay", 3, 1), ("rope", 1, 0), ("rope", 1, 1), ("ob", 2)],
-    6: [("oa", 6), ("oy", 6), ("of", 5), ("far", 1, 1), ("far", 2, 1), ("far", 3, 0), ("far", 3, 1), ("rope", 1, 2), ("rope", 1, 3), ("ob", 3)],
-    7: [("oa", 7), ("oy", 7), ("of", 6), ("ob", 4)],
-    8: [("oa", 8), ("oy", 8), ("of", 7), ("ob", 5)],
-    "sent": [("of", 8), ("ob", 6)],
+    3: [("oa", 3), ("oy", 3), ("of", 2), ("hub", 3, 1), ("relay", 1, 0), ("relay", 2, 0), ("far", 0, 0), ("far", 0, 1), ("rope", 0, 0), ("rope", 0, 1), ("ob", 1)],
+    4: [("oa", 4), ("oy", 4), ("of", 3), ("relay", 1, 1), ("relay", 2, 1), ("far", 1, 0), ("far", 2, 0), ("rope", 0, 2), ("rope", 0, 3), ("ob", 2)],
+    5: [("oa", 5), ("oy", 5), ("of", 4), ("relay", 3, 0), ("relay", 3, 1), ("rope", 1, 0), ("rope", 1, 1), ("ob", 3)],
+    6: [("oa", 6), ("oy", 6), ("of", 5), ("far", 1, 1), ("far", 2, 1), ("far", 3, 0), ("far", 3, 1), ("rope", 1, 2), ("rope", 1, 3), ("ob", 4)],
+    7: [("oa", 7), ("oy", 7), ("of", 6), ("ob", 5)],
+    8: [("oa", 8), ("oy", 8), ("of", 7), ("ob", 6)],
+    "sent": [("of", 8)],
     "back": [("ob", 7)],
     "first": [("ob", 8)],
 }
@@ -45,8 +45,8 @@
 
 def kernel(
     hidden_ref, cache_ref, lens_ref, gain_ref, wq_ref, bias_ref, wo_ref, freq_ref, out_ref,
-    gain, bias, lens, freq, hid, cache, hg, xs, wq, wo, ssb, ps, pr, osb, orb, xsb, xrb, qs, sc, mx, rope_c, rope_s, rcol, acc,
-    loc_sem, h1, hx, hs, hh, hsend, zs, zsend, ss_sem, rs, rss, oa, ob, oby, oyf, oy, osend, od, ods, xr, xss,
+    gain, bias, lens, freq, hid, cache, hg, xs, wq, wo, ssb, ps, pr, rf, osb, orb, xsb, xrb, xf, qs, sc, mx, rope_c, rope_s, rcol, acc,
+    loc_sem, h1, hx, hs, hh, hsend, zs, zsend, ss_sem, rs, rss, rfs, oa, ob, oby, oyf, oy, osend, od, ods, xr, xss, xfs,
 ):
     g, d, t = lax.axis_index("group"), lax.axis_index("dp"), lax.axis_index("tensor")
     y, z = lax.rem(g, 4), (g // 4) * 8 + d
@@ -304,18 +304,40 @@
     def rows_of(h):
         return slice(h * HTOK, (h + 1) * HTOK)
 
-    def r_send(j, dy, h):
-        rows = pl.ds(h * HTOK, HTOK)
-        send(ps.at[j, rows], pr.at[j, rows], rss.at[j, h], rs.at[j, h], dev(dy=dy))
-
-    ways = ((0, 2), (1, 1), (2, 3))
-    for j, dy in ways:
-        ps[j] = product(lax.rem(y + dy, NY)).astype(BF)
-        r_send(j, dy, 0)
-    for j, dy in ways:
-        r_send(j, dy, 1)
+    quarter = HTOK // 2
+
+    def r_rows(h, sub):
+        return pl.ds(h * HTOK + sub * quarter, quarter)
+
+    def r_far(h):
+        for way, dy in ((0, 1), (1, -1)):
+            part = ps.at[2, r_rows(h, way)]
+            send(part, rf.at[way, h], rss.at[2, h, way], rfs.at[way, h], dev(dy=dy))
+
+    def r_near(h, way, sub):
+        rows = r_rows(h, sub)
+        send(ps.at[way, rows], pr.at[way, rows], rss.at[way, h, sub], rs.at[way, h, sub], dev(dy=1 if way == 0 else -1))
+
+    def r_join(h):
+        for way in (0, 1):
+            rows = slice(h * HTOK + way * quarter, h * HTOK + (way + 1) * quarter)
+            wait(rf.at[way, h], rfs.at[way, h])
+            ps[way, rows] = (ps[way, rows].astype(F32) + rf[way, h].astype(F32)).astype(BF)
+            r_near(h, way, way)
+
+    ps[2] = product(lax.rem(y + 2, NY)).astype(BF)
+    r_far(0)
+    ps[0] = product(lax.rem(y + 1, NY)).astype(BF)
+    r_near(0, 0, 1)
+    ps[1] = product(lax.rem(y + 3, NY)).astype(BF)
+    r_near(0, 1, 0)
+    r_far(1)
     acc[...] = product(y)
+    r_join(0)
+    for way in (0, 1):
+        r_near(1, way, 1 - way)
     run("sent")
+    r_join(1)
 
     wait(ssb.at[0:7], ss_sem.at[1])
     whole = jnp.sum(ssb[...], axis=0)[0:1, :] * (1.0 / (8 * FEAT))
@@ -343,14 +365,15 @@
 
     def attention(h):
         rows = rows_of(h)
-        for j in (1, 2, 0):
-            wait(pr.at[j, pl.ds(h * HTOK, HTOK)], rs.at[j, h])
+        for sub in (0, 1):
+            for way in (0, 1):
+                wait(pr.at[way, r_rows(h, sub)], rs.at[way, h, sub])
 
         def head(i):
             cols = slice(i * HD, (i + 1) * HD)
             total = acc[rows, cols]
-            for j in range(3):
-                total += pr[j, rows, cols].astype(F32)
+            for way in (0, 1):
+                total += pr[way, rows, cols].astype(F32)
             return total * rcol[rows, :] + bias[i : i + 1, :]
 
         def rotate(v):
@@ -399,6 +422,20 @@
         block = wo[pl.ds(index * 8, 8)].reshape(8 * DEEP, OUTC)
         return lax.dot_general(mixed, block, NT, preferred_element_type=F32)
 
+    def x_near(h, way, sub):
+        rows = r_rows(h, sub)
+        send(
+            xsb.at[1 + way, rows], xrb.at[way, rows], xss.at[1 + way, h, sub], xr.at[way, h, sub],
+            dev(dx=1 if way == 0 else -1),
+        )
+
+    def x_join(h):
+        for way in (0, 1):
+            rows = slice(h * HTOK + way * quarter, h * HTOK + (way + 1) * quarter)
+            wait(xf.at[way, h], xfs.at[way, h])
+            xsb[1 + way, rows] = (xsb[1 + way, rows].astype(F32) + xf[way, h].astype(F32)).astype(BF)
+            x_near(h, way, way)
+
     def outputs(h, mixed):
         rows, there = rows_of(h), pl.ds(h * HTOK, HTOK)
         for j, dx in enumerate((2, 1, 3, 0)):
@@ -410,17 +447,22 @@
             total += orb[j, rows].astype(F32)
             if j < 3:
                 xsb[j, rows] = total.astype(BF)
-                send(xsb.at[j, there], xrb.at[j, there], xss.at[j, h], xr.at[j, h], dev(dx=dx))
             else:
                 acc[rows, :] = total
+            if j == 0:
+                for way, step in ((0, 1), (1, -1)):
+                    send(xsb.at[0, r_rows(h, way)], xf.at[way, h], xss.at[0, h, way], xfs.at[way, h], dev(dx=step))
+            elif j < 3:
+                x_near(h, j - 1, 2 - j)
 
     def finish(h):
         rows = rows_of(h)
-        for j in (1, 2, 0):
-            wait(xrb.at[j, pl.ds(h * HTOK, HTOK)], xr.at[j, h])
+        for sub in (0, 1):
+            for way in (0, 1):
+                wait(xrb.at[way, r_rows(h, sub)], xr.at[way, h, sub])
         total = acc[rows, :]
-        for j in range(3):
-            total += xrb[j, rows].astype(F32)
+        for way in (0, 1):
+            total += xrb[way, rows].astype(F32)
         hid[:, h * HALF : (h + 1) * HALF, :] = total.astype(BF).reshape(STEPS, HALF, FEAT)
 
     mixed = attention(0)
@@ -428,7 +470,9 @@
     wait(wo.at[0:32, pl.ds(0, ACUT)], oy)
     outputs(0, mixed)
     mixed = attention(1)
+    x_join(0)
     outputs(1, mixed)
+    x_join(1)
     finish(0)
     finish(1)
     back = pltpu.make_async_copy(hid, out_ref, loc_sem.at[0])
@@ -457,8 +501,9 @@
     for h in (0, 1):
         there = pl.ds(h * HTOK, HTOK)
         for j in range(3):
-            wait(ps.at[j, there], rss.at[j, h])
-            wait(xsb.at[j, there], xss.at[j, h])
+            for sub in (0, 1):
+                wait(ps.at[j, r_rows(h, sub)], rss.at[j, h, sub])
+                wait(xsb.at[j, r_rows(h, sub)], xss.at[j, h, sub])
         for j in range(4):
             wait(osb.at[j, there], ods.at[j, h])
     back.wait()
@@ -489,11 +534,13 @@
             pltpu.VMEM((NY * NZ, DEEP, OUTC), BF),
             pltpu.VMEM((8, 8, TOK), F32),
             pltpu.VMEM((3, TOK, FEAT), BF),
-            pltpu.VMEM((3, TOK, FEAT), BF),
+            pltpu.VMEM((2, TOK, FEAT), BF),
+            pltpu.VMEM((2, 2, HTOK // 2, FEAT), BF),
             pltpu.VMEM((4, TOK, FEAT), BF),
             pltpu.VMEM((4, TOK, FEAT), BF),
             pltpu.VMEM((3, TOK, FEAT), BF),
-            pltpu.VMEM((3, TOK, FEAT), BF),
+            pltpu.VMEM((2, TOK, FEAT), BF),
+            pltpu.VMEM((2, 2, HTOK // 2, FEAT), BF),
             pltpu.VMEM((nq, HD), F32),
             pltpu.VMEM((nq, HD), F32),
             pltpu.VMEM((nq, HD), F32),
@@ -510,8 +557,9 @@
             dma((2, 8, len(ZCUTS))),
             dma,
             dma((2,)),
-            dma((3, 2)),
-            dma((3, 2)),
+            dma((2, 2, 2)),
+            dma((3, 2, 2)),
+            dma((2, 2)),
             dma((2, 8)),
             dma((2, 4, 8)),
             dma((4,)),
@@ -520,8 +568,9 @@
             dma,
             dma((4, 2)),
             dma((4, 2)),
-            dma((3, 2)),
-            dma((3, 2)),
+            dma((2, 2, 2)),
+            dma((3, 2, 2)),
+            dma((2, 2)),
         ],
         compiler_params=pltpu.CompilerParams(
             collective_id=0, has_side_effects=True, vmem_limit_bytes=56 * 2**20

time: 92.6 us -> 90 us (0.972)
  Pallas kernels: 90.7 us -> 88.2 us
    pallas_call x1, Pallas kernels: 90.7 us -> 88.2 us  [on_device(): pl.pallas_call(kernel, out_shape=jax.ShapeDtypeStruct((STEPS, ROWS, FEAT)...]
where the time goes in v3:
time: 90 us; the launch traced here: 89.9 us
  Pallas kernels  88.2 us (98%)
  local copies, waits for them, and re-layouts  1.73 us (2%)
    pallas_call x1, Pallas kernels, on_device(): pl.pallas_call(kernel, out_shape=jax.ShapeDtypeStruct((STEPS, ROWS, FEAT)...  88.2 us

profile of v3, /device:TPU:1, one launch (start us, length us, event | category | flops | bytes accessed | tf_op | source)
XLA Modules:
  0.0 89.9 jit_solution(11461948718127883860)
XLA Ops:
  0.0 88.2 %shard_map.82 = bf16[4,64,640]{2,1,0:T(8,128)(2,1)} custom-call(bf16[4,64,640]{2,1,0:T(8,128)(2,1)} %hidden_ref.1, bf16[64,128,256]{2,1,0:T(8,128)(2,1)} %bitcast.4, s32[1,64]{1,0:T(1,128)} %bitcast.7, f32[40,128]{1,0:T(8,128)} %bitcast.5, bf16[80,640]{1,0:T(8,128)(2,1)} %wq_ref.1, f32[5,128]{1,0:T(8,128)} %bitcast.6, bf16[80,384]{1,0:T(8,128)(2,1)} %wo_ref.1, ...), custom_call_target="tpu_custom_call" | custom-call | tf_op jit(solution)/shard_map/pallas_call | solution.py:519
  88.2 1.7 %copy.10 = bf16[4,64,640]{2,1,0:T(8,128)(2,1)} copy(bf16[4,64,640]{2,1,0:T(8,128)(2,1)} %shard_map.82) | data formatting | bytes 655360

commit v4 on v3

--- a/solution.py
+++ b/solution.py
@@ -438,10 +438,14 @@
 
     def outputs(h, mixed):
         rows, there = rows_of(h), pl.ds(h * HTOK, HTOK)
-        for j, dx in enumerate((2, 1, 3, 0)):
+        def give(j, dx):
             osb[j, rows] = partial_out(mixed, 2 * lax.rem(x + dx, NX) + 1 - c).astype(BF)
             send(osb.at[j, there], orb.at[j, there], ods.at[j, h], od.at[j, h], dev(flip=True))
-        for j, dx in enumerate((2, 1, 3, 0)):
+        steps = (2, 1, 3, 0)
+        give(0, steps[0])
+        for j, dx in enumerate(steps):
+            if j < 3:
+                give(j + 1, steps[j + 1])
             total = partial_out(mixed, 2 * lax.rem(x + dx, NX) + c)
             wait(orb.at[j, there], od.at[j, h])
             total += orb[j, rows].astype(F32)

time: 90 us -> 91.8 us (1.020)
  Pallas kernels: 88.2 us -> 89.9 us
    pallas_call x1, Pallas kernels: 88.2 us -> 89.9 us  [on_device(): pl.pallas_call(kernel, out_shape=jax.ShapeDtypeStruct((STEPS, ROWS, FEAT)...]
where the time goes in v4:
time: 91.8 us; the launch traced here: 91.6 us
  Pallas kernels  89.9 us (98%)
  local copies, waits for them, and re-layouts  1.73 us (2%)
    pallas_call x1, Pallas kernels, on_device(): pl.pallas_call(kernel, out_shape=jax.ShapeDtypeStruct((STEPS, ROWS, FEAT)...  89.9 us

profile of v4, /device:TPU:1, one launch (start us, length us, event | category | flops | bytes accessed | tf_op | source)
XLA Modules:
  0.0 91.6 jit_solution(8844676372335641132)
XLA Ops:
  0.0 89.9 %shard_map.82 = bf16[4,64,640]{2,1,0:T(8,128)(2,1)} custom-call(bf16[4,64,640]{2,1,0:T(8,128)(2,1)} %hidden_ref.1, bf16[64,128,256]{2,1,0:T(8,128)(2,1)} %bitcast.4, s32[1,64]{1,0:T(1,128)} %bitcast.7, f32[40,128]{1,0:T(8,128)} %bitcast.5, bf16[80,640]{1,0:T(8,128)(2,1)} %wq_ref.1, f32[5,128]{1,0:T(8,128)} %bitcast.6, bf16[80,384]{1,0:T(8,128)(2,1)} %wo_ref.1, ...), custom_call_target="tpu_custom_call" | custom-call | tf_op jit(solution)/shard_map/pallas_call | solution.py:523
  89.9 1.7 %copy.10 = bf16[4,64,640]{2,1,0:T(8,128)(2,1)} copy(bf16[4,64,640]{2,1,0:T(8,128)(2,1)} %shard_map.82) | data formatting | bytes 655360
